TPU v7x, 256 devices: a whole 4x4x8 slice. The times are simulated.
256 devices in a mesh: outer: 8 (over y, x_hi), dp: 16 (over z, core), tensor: 2 (over x_lo).
Axes of the slice: x: 4 (x_hi: 2, x_lo: 2; x = x_hi * 2 + x_lo), y: 4, z: 8, core: 2. Of those that a mesh axis runs over, the one named last changes fastest.
Arguments:
- attn_out: bfloat16 [16384, 8192], P(('outer', 'dp')), may hold values from -24 to 24
- cotangent: bfloat16 [16384, 4096], P(('outer', 'dp'), 'tensor'), may hold values from -10 to 10
- out_weight: bfloat16 [8192, 4096], P('dp', 'tensor'), may hold values from -0.09375 to 0.09375
Outputs:
- input_grad: bfloat16 [16384, 8192], P(('outer', 'dp'))
- weight_grad: bfloat16 [8192, 4096], P('dp', 'tensor')
All inputs are finite; a program needn't handle non-finite values.
Results may differ from a plain program's by a relative error of at most 0.018.
Values may be sent and summed in bfloat16 or wider, within the bound.
A program may use at most 64 MiB of HBM per device.

v0:
```python
import math

import jax
import jax.numpy as jnp
from jax import lax
from jax.sharding import PartitionSpec as P

BLOCK = 128


clip_ratio = 2.5


def hadamard(length):
    numbers = jnp.arange(length, dtype=jnp.int32)
    common = jnp.bitwise_and(numbers[:, None], numbers[None, :])
    parity = jnp.zeros_like(common)
    for position in range(int(length).bit_length()):
        parity = parity + jnp.bitwise_and(jnp.right_shift(common, position), 1)
    signs_table = 1.0 - 2.0 * jnp.bitwise_and(parity, 1).astype(jnp.float32)
    return signs_table / math.sqrt(length)


def rotate(matrix, table):
    height = matrix.shape[0]
    blocks = matrix.reshape(height, -1, table.shape[0])
    turned = jnp.einsum("rbk,kj->rbj", blocks, table, precision=lax.Precision.HIGHEST)
    return turned.reshape(height, -1)


def clip_blocks(matrix, width):
    height = matrix.shape[0]
    blocks = matrix.reshape(height, -1, width)
    mean_square = jnp.mean(blocks * blocks, axis=-1, keepdims=True)
    limit = clip_ratio * jnp.sqrt(mean_square + 1e-06)
    return jnp.clip(blocks, -limit, limit).reshape(height, -1)


def local(attn_out, cotangent, out_weight):
    table = hadamard(BLOCK)
    tokens_all = attn_out.shape[0] * lax.axis_size("outer") * lax.axis_size("dp")
    factor = tokens_all ** (-0.5)
    act_block = lax.all_to_all(attn_out, "dp", split_axis=1, concat_axis=0, tiled=True)
    cot_pod = lax.all_gather(cotangent, "dp", axis=0, tiled=True)
    partial_value = lax.dot_general(
        cot_pod, out_weight, (((1,), (1,)), ((), ())), preferred_element_type=jnp.float32
    )
    summed = lax.psum(partial_value.astype(jnp.bfloat16), "tensor")
    input_grad = lax.all_to_all(summed, "dp", split_axis=0, concat_axis=1, tiled=True)
    pod_grad = (
        lax.dot_general(
            act_block, cot_pod, (((0,), (0,)), ((), ())), preferred_element_type=jnp.float32
        )
        * factor
    )
    rotated = clip_blocks(rotate(pod_grad, table), BLOCK)
    total = lax.psum(rotated.astype(jnp.bfloat16), "outer").astype(jnp.float32)
    weight_grad = rotate(total, table).astype(jnp.bfloat16)
    return (input_grad, weight_grad)


def solution(mesh):
    in_specs = (P(("outer", "dp"), None), P(("outer", "dp"), "tensor"), P("dp", "tensor"))
    out_specs = (P(("outer", "dp"), None), P("dp", "tensor"))
    return jax.shard_map(local, mesh=mesh, in_specs=in_specs, out_specs=out_specs, check_vma=False)
```

profile of v0, /device:TPU:1, one launch (start us, length us, event | category | flops | bytes accessed | tf_op | source)
XLA Modules:
  0.0 346.6 jit_solution(7213190533713195691)
XLA Ops:
  7.2 0.0 copy-start
  7.2 0.0 all-gather.2.cloned.1.call-start
  7.2 0.7 all-gather.2.cloned.1.call-update
  7.9 4.1 %copy.14 = bf16[128,8192]{0,1:T(8,128)(2,1)} copy(bf16[128,8192]{1,0:T(8,128)(2,1)} %param.3) | data formatting | bytes 4194304 | tf_op args[0]
  12.0 10.0 %all-to-all-start.1 = ((bf16[128,16,512]{0,2,1:T(8,128)(2,1)}), bf16[128,16,512]{0,2,1:T(8,128)(2,1)}, u32[]{:S(2)}, u32[]{:S(2)}) async-start(bf16[128,16,512]{0,2,1:T(8,128)(2,1)} %bitcast.27), calls=%async_computation.1 | async-start | bytes 4194304 | tf_op jit(solution)/shard_map/all_to_all | solution.py:43
  22.0 0.0 all-reduce.3.cloned.1.call-start
  22.0 90.1 %all-gather.2.cloned.1.call-done = bf16[2048,2048]{1,0:T(8,128)(2,1)} async-done(((bf16[128,2048]{1,0:T(8,128)(2,1)}), bf16[2048,2048]{1,0:T(8,128)(2,1)}) %all-gather.2.cloned.1.call-update) | async-done | bytes 8388624 | tf_op jit(solution)/shard_map/all_gather | solution.py:44
  112.1 0.0 copy-done
  112.1 9.1 %convolution_convert_fusion = bf16[2048,512]{1,0:T(8,128)(2,1)} fusion(bf16[2048,2048]{1,0:T(8,128)(2,1)} %all-gather.2.cloned.1.call-done, bf16[512,2048]{1,0:T(8,128)(2,1)S(1)} %copy-done), kind=kOutput, calls=%fused_computation.6 | convolution fusion | flops 4296015872 | bytes 12582912 | tf_op jit(solution)/shard_map/dot_general | solution.py:45
  121.3 0.0 all-reduce.3.cloned.1.call-update
  121.3 0.0 all-to-all-done.1
  121.3 3.9 %copy.15 = bf16[16,128,512]{2,1,0:T(8,128)(2,1)} copy(bf16[16,128,512]{1,2,0:T(8,128)(2,1)} %bitcast.3) | data formatting | bytes 4194304 | tf_op jit(solution)/shard_map/all_to_all | solution.py:43
  125.2 69.5 %all-reduce.3.cloned.1.call-done = bf16[16,128,512]{2,1,0:T(8,128)(2,1)} async-done(((bf16[16,128,512]{2,1,0:T(8,128)(2,1)}), bf16[16,128,512]{2,1,0:T(8,128)(2,1)}) %all-reduce.3.cloned.1.call-update) | async-done | bytes 2097168 | tf_op jit(solution)/shard_map/psum | solution.py:48
  194.7 7.7 %all-to-all-start = ((bf16[16,128,512]{2,1,0:T(8,128)(2,1)}), bf16[16,128,512]{2,1,0:T(8,128)(2,1)}, u32[]{:S(2)}, u32[]{:S(2)}) async-start(bf16[16,128,512]{2,1,0:T(8,128)(2,1)} %all-reduce.3.cloned.1.call-done), calls=%async_computation | async-start | bytes 4194304 | tf_op jit(solution)/shard_map/all_to_all | solution.py:49
  202.4 0.2 all-reduce.5.cloned.1.call-start
  202.6 7.6 %multiply_bitcast_fusion = f32[64,16,8,128]{3,2,1,0:T(8,128)S(1)} fusion(bf16[2048,512]{1,0:T(8,128)(2,1)} %bitcast.30, bf16[2048,2048]{1,0:T(8,128)(2,1)} %all-gather.2.cloned.1.call-done), kind=kOutput, calls=%fused_computation.5 | convolution fusion | flops 4296015872 | bytes 14680064 | tf_op jit(solution)/shard_map/dot_general | solution.py:51
  210.3 4.2 %multiply_reduce_fusion = (f32[512,16]{0,1:T(8,128)S(1)}, bf16[512,16,128]{0,2,1:T(8,128)(2,1)S(1)}) fusion(f32[64,16,8,128]{3,2,1,0:T(8,128)S(1)} %multiply_bitcast_fusion), kind=kOutput, calls=%fused_computation.4 | convolution fusion | flops 1614225408 | bytes 6324224 | tf_op jit(solution)/shard_map/rbk,kj->rbj/dot_general | solution.py:27
  214.5 1.5 minimum_convert_fusion
  216.0 0.0 all-reduce.5.cloned.1.call-update
  216.0 112.3 %all-reduce.5.cloned.1.call-done = bf16[512,16,128]{0,2,1:T(8,128)(2,1)} async-done(((bf16[512,16,128]{0,2,1:T(8,128)(2,1)}), bf16[512,16,128]{0,2,1:T(8,128)(2,1)}) %all-reduce.5.cloned.1.call-update) | async-done | bytes 2097168 | tf_op jit(solution)/shard_map/psum | solution.py:57
  328.3 4.7 %convolution_convert_fusion.1 = bf16[512,16,128]{0,2,1:T(8,128)(2,1)} fusion(bf16[512,16,128]{0,2,1:T(8,128)(2,1)} %all-reduce.5.cloned.1.call-done), kind=kOutput, calls=%fused_computation.7 | convolution fusion | flops 1612136448 | bytes 4194304 | tf_op jit(solution)/shard_map/rbk,kj->rbj/dot_general | solution.py:27
  333.0 3.9 %copy.18 = bf16[512,2048]{1,0:T(8,128)(2,1)} copy(bf16[512,2048]{0,1:T(8,128)(2,1)} %bitcast.28) | data formatting | bytes 4194304
  337.0 0.0 all-to-all-done
  337.0 3.1 copy.21
  (1 shorter events, 0.0 us)
Async XLA Ops:
  7.2 105.0 %copy-start = (bf16[512,2048]{1,0:T(8,128)(2,1)S(1)}, bf16[512,2048]{1,0:T(8,128)(2,1)}, u32[]{:S(2)}) copy-start(bf16[512,2048]{1,0:T(8,128)(2,1)} %param.5) | copy-start | bytes 6291460
  7.2 105.0 %all-gather.2.cloned.1.call-start = ((), (), s32[]{:S(2)}) async-start(), calls=%async_computation.2 | async-start | bytes 8912896 | tf_op jit(solution)/shard_map/all_gather | solution.py:44
  12.0 109.3 %all-to-all-start.1 = ((bf16[128,16,512]{0,2,1:T(8,128)(2,1)}), bf16[128,16,512]{0,2,1:T(8,128)(2,1)}, u32[]{:S(2)}, u32[]{:S(2)}) async-start(bf16[128,16,512]{0,2,1:T(8,128)(2,1)} %bitcast.27), calls=%async_computation.1 | async-start | bytes 4194304 | tf_op jit(solution)/shard_map/all_to_all | solution.py:43
  22.0 172.7 %all-reduce.3.cloned.1.call-start = ((), (), s32[]{:S(2)}) async-start(), calls=%async_computation.3 | async-start | bytes 4194304 | tf_op jit(solution)/shard_map/psum | solution.py:48
  194.7 142.2 %all-to-all-start = ((bf16[16,128,512]{2,1,0:T(8,128)(2,1)}), bf16[16,128,512]{2,1,0:T(8,128)(2,1)}, u32[]{:S(2)}, u32[]{:S(2)}) async-start(bf16[16,128,512]{2,1,0:T(8,128)(2,1)} %all-reduce.3.cloned.1.call-done), calls=%async_computation | async-start | bytes 4194304 | tf_op jit(solution)/shard_map/all_to_all | solution.py:49
  202.4 125.9 %all-reduce.5.cloned.1.call-start = ((), (), s32[]{:S(2)}) async-start(), calls=%async_computation.4 | async-start | bytes 4194304 | tf_op jit(solution)/shard_map/psum | solution.py:57
Sparse Core Ops, SparseCore 0:
  9.8 102.2 all-gather.1
  121.4 73.2 all-reduce.2
  216.2 112.0 all-reduce.4
where the time goes:
time: 347 us
  waiting for transfers between devices  273 us (79%)
  matrix products  25.7 us (7%)
  starting transfers between devices  18 us (5%)
  local copies, waits for them, and re-layouts  15 us (4%)
  between operations  13.8 us (4%)
    psum x1, waiting for transfers between devices, local(): total = lax.psum(rotated.astype(jnp.bfloat16), 'outer').astype(jnp.float32)  112 us
    all_gather x1, waiting for transfers between devices, local(): cot_pod = lax.all_gather(cotangent, 'dp', axis=0, tiled=True)  90.1 us
    psum x1, waiting for transfers between devices, local(): summed = lax.psum(partial_value.astype(jnp.bfloat16), 'tensor')  69.5 us
    all_to_all x1, starting transfers between devices, local(): lax.all_to_all(attn_out, 'dp', split_axis=1, concat_axis=0, tiled=True)  9.98 us
    dot_general x1, matrix products, local(): lax.dot_general(cot_pod, out_weight, (((1,), (1,)), ((), ())), preferred_...  9.15 us
    dot_general x2, matrix products, rotate(): jnp.einsum('rbk,kj->rbj', blocks, table, precision=lax.Precision.HIGHEST)  8.96 us
    unnamed x4, local copies, waits for them, and re-layouts  7.99 us
    all_to_all x1, starting transfers between devices, local(): lax.all_to_all(summed, 'dp', split_axis=0, concat_axis=1, tiled=True)  7.7 us
  transfers between devices with their start and end apart: 5, of which 3 were waited for; matrix products, arithmetic and copies ran while one was open for 11% of the time, Pallas kernels for 0%

commit v1 on v0

v1 whole, which is shorter than its diff:
```python
import functools

import jax
import jax.numpy as jnp
from jax import lax
from jax.experimental import pallas as pl
from jax.experimental.pallas import tpu as pltpu
from jax.sharding import PartitionSpec as P

MESH = pl.DeviceIdType.MESH
F32, BF16 = jnp.float32, jnp.bfloat16
NZ = 8
BLOCK = 128
TOK = 128
DCOL = 2048
HROW = 512
HALF = 256
CLIP = 2.5


def signs():
    row = lax.broadcasted_iota(jnp.int32, (BLOCK, BLOCK), 0)
    col = lax.broadcasted_iota(jnp.int32, (BLOCK, BLOCK), 1)
    common = row & col
    common = common ^ (common >> 4)
    common = common ^ (common >> 2)
    common = common ^ (common >> 1)
    return (1 - 2 * (common & 1)).astype(F32).astype(BF16)


def dot(a, b):
    return jnp.dot(a, b, preferred_element_type=F32)


def kernel(attn, cot, w, out, outw, COT, WV, WRT, ACT, AT, PART, PSEND, PRECV, OSEND, WG, RS1, RS2, RSX, S2, SX, FIN,
           ring_s, ring_r, sib_s, sib_r, att_s, att_r, arl_s, arl_r, par_s, par_r, out_s, out_r, orl_s, orl_r,
           rs_s, rs_r, ag_s, ag_r, loc):
    outer, me, t = lax.axis_index("outer"), lax.axis_index("dp"), lax.axis_index("tensor")
    z, c = me // 2, me % 2
    y, xh = outer // 2, outer % 2
    sib = z * 2 + 1 - c
    b1 = (y % 2 + y // 2) % 2
    b2 = y // 2
    y1 = y + 1 - 2 * (y % 2)
    y3 = 3 - y
    factor = (TOK * 2 * NZ * 8) ** (-0.5)

    def remote(src, dst, ssem, rsem, where):
        return pltpu.make_async_remote_copy(
            src_ref=src, dst_ref=dst, send_sem=ssem, recv_sem=rsem, device_id=where, device_id_type=MESH)

    def zdev(k):
        return {"dp": k}

    peer = {"tensor": 1 - t}

    def zat(dz):
        return (z + dz + 2 * NZ) % NZ

    def rows(ref, at, count, unit=None):
        return ref.at[pl.ds(pl.multiple_of(at, unit or count), count), :]

    barrier = pltpu.get_barrier_semaphore()

    def greet(k, carry):
        pl.semaphore_signal(barrier, inc=1, device_id={"dp": (me + k) % (2 * NZ)}, device_id_type=MESH)
        return carry

    lax.fori_loop(1, 2 * NZ, greet, 0)
    pl.semaphore_signal(barrier, inc=1, device_id=peer, device_id_type=MESH)
    for where in (y1 * 2 + xh, y3 * 2 + xh, y * 2 + 1 - xh):
        pl.semaphore_signal(barrier, inc=1, device_id={"outer": where}, device_id_type=MESH)

    load_w = pltpu.make_async_copy(w, WV, loc.at[0])
    load_w.start()
    own_act = pltpu.make_async_copy(
        attn.at[:, pl.ds(pl.multiple_of(me * HROW, HROW), HROW)], rows(ACT, me * TOK, TOK), loc.at[1])
    own_act.start()

    S = signs()
    for b in range(DCOL // BLOCK):
        part = slice(b * BLOCK, (b + 1) * BLOCK)
        COT[pl.ds(pl.multiple_of(me * TOK, TOK), TOK), part] = (dot(cot[:, part], S) * 0.125).astype(BF16)

    pl.semaphore_wait(barrier, 2 * NZ - 1 + 4)

    def ring(direction, step, half):
        sgn = 1 - 2 * direction
        block = rows(COT, (zat(-sgn * step) * 2 + c) * TOK + half * 64, 64)
        at = direction * 8 + step * 2 + half
        return remote(block, block, ring_s.at[at], ring_r.at[at], zdev(zat(sgn) * 2 + c))

    def ring_in(direction, step, half):
        sgn = 1 - 2 * direction
        block = rows(COT, (zat(-sgn * (step + 1)) * 2 + c) * TOK + half * 64, 64)
        at = direction * 8 + step * 2 + half
        return remote(block, block, ring_s.at[at], ring_r.at[at], zdev(zat(sgn) * 2 + c))

    LAST = ((0, 0), (1, 1))

    def sib_copy(dz, core):
        at = dz % NZ
        block = rows(COT, (zat(dz) * 2 + core) * TOK, TOK)
        return remote(block, block, sib_s.at[at], sib_r.at[at], zdev(sib))

    def other(k, dz):
        return zat((1 - 2 * (k // 2)) * dz) * 2 + k % 2

    def count(dz):
        return 2 if dz == NZ // 2 else 4

    def att_copy(to):
        src = attn.at[pl.ds(pl.multiple_of(t * 64, 64), 64), pl.ds(pl.multiple_of(to * HROW, HROW), HROW)]
        return remote(src, rows(ACT, me * TOK + t * 64, 64), att_s.at[to], att_r.at[me], zdev(to))

    def att_in(j):
        block = rows(ACT, j * TOK + t * 64, 64)
        return remote(block, block, att_s.at[j], att_r.at[j], zdev(j))

    def arl_copy(j):
        block = rows(ACT, j * TOK + t * 64, 64)
        return remote(block, block, arl_s.at[j], arl_r.at[j], peer)

    def arl_in(j):
        block = rows(ACT, j * TOK + (1 - t) * 64, 64)
        return remote(block, block, arl_s.at[j], arl_r.at[j], peer)

    def sib_att():
        return remote(attn.at[:, pl.ds(pl.multiple_of(sib * HROW, HROW), HROW)], rows(ACT, me * TOK, TOK),
                      att_s.at[sib], att_r.at[me], zdev(sib))

    def sib_att_in():
        block = rows(ACT, sib * TOK, TOK)
        return remote(block, block, att_s.at[sib], att_r.at[sib], zdev(sib))

    def over(dz, body):
        def step(k, carry):
            body(other(k, dz))
            return carry
        lax.fori_loop(0, count(dz), step, 0)

    def att_send(dz):
        over(dz, lambda j: att_copy(j).start())

    def att_relay(dz):
        def body(j):
            att_in(j).wait_recv()
            arl_copy(j).start()
        over(dz, body)

    def turn(j):
        AT[:, pl.ds(pl.multiple_of(j * TOK, TOK), TOK)] = ACT[pl.ds(pl.multiple_of(j * TOK, TOK), TOK), :].T

    def att_finish(dz):
        def body(j):
            arl_in(j).wait_recv()
            turn(j)
        over(dz, body)

    def par_copy(zz):
        return remote(rows(PSEND, zz * HALF, HALF), rows(PRECV, zz * HALF, HALF), par_s.at[zz], par_r.at[zz], peer)

    def process(zz):
        at = pl.ds(pl.multiple_of(zz * HALF, HALF), HALF)
        x = COT[at, :]
        PSEND[at, :] = dot(x, WRT[:, pl.ds(pl.multiple_of((1 - t) * HALF, HALF), HALF)]).astype(BF16)
        par_copy(zz).start()
        PART[at, :] = dot(x, WRT[:, pl.ds(pl.multiple_of(t * HALF, HALF), HALF)])

    def mine(j):
        return out.at[:, pl.ds(pl.multiple_of(j * HROW + t * HALF, HALF), HALF)]

    def theirs(j):
        return out.at[:, pl.ds(pl.multiple_of(j * HROW + (1 - t) * HALF, HALF), HALF)]

    def out_copy(to):
        return remote(rows(OSEND, to * TOK, TOK), mine(me), out_s.at[to], out_r.at[me], zdev(to))

    def out_in(j):
        return remote(mine(j), mine(j), out_s.at[j], out_r.at[j], zdev(j))

    def orl_copy(j, src=None):
        return remote(mine(j) if src is None else src, mine(j), orl_s.at[j], orl_r.at[j], peer)

    def orl_in(j):
        return remote(theirs(j), theirs(j), orl_s.at[j], orl_r.at[j], peer)

    own_out = pltpu.make_async_copy(rows(OSEND, me * TOK, TOK), mine(me), loc.at[2])

    def out_sum(zz):
        par_copy(zz).wait_recv()
        at = pl.ds(pl.multiple_of(zz * HALF, HALF), HALF)
        OSEND[at, :] = (PART[at, :] + PRECV[at, :].astype(F32)).astype(BF16)

    def out_stage(zz):
        out_sum(zz)
        out_copy(zz * 2).start()
        out_copy(zz * 2 + 1).start()

    def out_relay(dz):
        def body(j):
            out_in(j).wait_recv()
            orl_copy(j).start()
        over(dz, body)

    for half in range(2):
        for direction in range(2):
            ring(direction, 0, half).start()
    sib_copy(0, c).start()
    sib_att().start()
    att_send(4)

    load_w.wait()
    for b in range(DCOL // BLOCK):
        part = slice(b * BLOCK, (b + 1) * BLOCK)
        turned = lax.dot_general(S, WV[:, part], (((0,), (1,)), ((), ())), preferred_element_type=F32)
        WRT[part, :] = (turned * 0.0625).astype(BF16)
    sib_copy(0, 1 - c).wait_recv()
    process(z)
    own_act.wait()
    turn(me)

    for step in range(1, 4):
        for half in range(2):
            for direction in range(2):
                ring_in(direction, step - 1, half).wait_recv()
                if step < 3 or (direction, half) in LAST:
                    ring(direction, step, half).start()
        sib_copy(-step, c).start()
        sib_copy(step, c).start()
        att_send(4 - step)
        att_relay(5 - step)
        if step == 1:
            sib_att_in().wait_recv()
            turn(sib)
        else:
            att_finish(6 - step)
        sib_copy(-step, 1 - c).wait_recv()
        process(zat(-step))
        sib_copy(step, 1 - c).wait_recv()
        process(zat(step))

    for direction, half in LAST:
        ring_in(direction, 3, half).wait_recv()
    sib_copy(4, c).start()
    att_relay(1)
    out_sum(z)
    own_out.start()
    out_copy(sib).start()
    orl_copy(me, rows(OSEND, me * TOK, TOK)).start()
    att_finish(2)
    sib_copy(4, 1 - c).wait_recv()
    process(zat(4))
    for dz in (3, -3, 2, -2):
        out_stage(zat(dz))
    att_finish(1)

    ones = jnp.ones((BLOCK, BLOCK), BF16)
    scale = factor * 8.0 * BLOCK ** (-0.5)

    def weight(ch):
        def piece(n, carry):
            at = pl.multiple_of(n * 512, 512)
            acc = dot(AT[ch * HALF:(ch + 1) * HALF, :], COT[:, pl.ds(at, 512)]) * scale
            clipped = []
            for b in range(4):
                x = acc[:, b * BLOCK:(b + 1) * BLOCK]
                mean = dot((x * x).astype(BF16), ones) * (1.0 / BLOCK)
                limit = CLIP * jnp.sqrt(mean + 1e-6)
                clipped.append(jnp.clip(x, -limit, limit).astype(BF16))
            WG[ch * HALF:(ch + 1) * HALF, pl.ds(at, 512)] = jnp.concatenate(clipped, axis=1)
            return carry
        lax.fori_loop(0, DCOL // 512, piece, 0)

    def pick(half, a, b):
        return (1 - half) * a + half * b

    def place(i):
        half = i % 2
        p1, p2 = pick(half, y1, y3) * 2 + xh, pick(half, y3, y1) * 2 + xh
        return p1, p2, pick(half, b1, b2), pick(half, b2, b1), i * 128

    px = {"outer": y * 2 + 1 - xh}

    def ds16(at, n):
        return pl.ds(pl.multiple_of(at, 16), n)

    def rs1_copy(i):
        p1, p2, q1, q2, base = place(i)
        return remote(WG.at[ds16(base + (1 - q1) * 64, 64), :], RS1.at[ds16(i * 64, 64), :],
                      rs_s.at[i], rs_r.at[i], {"outer": p1})

    def rs2_copy(i):
        p1, p2, q1, q2, base = place(i)
        return remote(S2.at[ds16(i * 32, 32), :], RS2.at[ds16(i * 32, 32), :], rs_s.at[4 + i], rs_r.at[4 + i], {"outer": p2})

    def rsx_copy(i):
        return remote(SX.at[ds16(i * 16, 16), :], RSX.at[ds16(i * 16, 16), :], rs_s.at[8 + i], rs_r.at[8 + i], px)

    def combos(body):
        def step(i, carry):
            body(i)
            return carry
        lax.fori_loop(0, 4, step, 0)

    def stage2(i):
        p1, p2, q1, q2, base = place(i)
        rs1_copy(i).wait_recv()
        off = (1 - q2) * 32
        S2[ds16(i * 32, 32), :] = (WG[ds16(base + q1 * 64 + off, 32), :].astype(F32)
                                   + RS1[ds16(i * 64 + off, 32), :].astype(F32)).astype(BF16)
        rs2_copy(i).start()

    def three(i, row):
        p1, p2, q1, q2, base = place(i)
        return (WG[ds16(base + q1 * 64 + q2 * 32 + row, 16), :].astype(F32)
                + RS1[ds16(i * 64 + q2 * 32 + row, 16), :].astype(F32)
                + RS2[ds16(i * 32 + row, 16), :].astype(F32))

    def stage3(i):
        rs2_copy(i).wait_recv()
        SX[ds16(i * 16, 16), :] = three(i, (1 - xh) * 16).astype(BF16)
        rsx_copy(i).start()

    def ag_row(i, f1, f2, fx):
        p1, p2, q1, q2, base = place(i)
        a = q1 if f1 == 0 else 1 - q1
        b = q2 if f2 == 0 else 1 - q2
        d = xh if fx == 0 else 1 - xh
        return outw.at[ds16(base + a * 64 + b * 32 + d * 16, 16), :]

    KIND = ((0, 0, 0), (0, 0, 0), (0, 0, 0), (0, 0, 1), (0, 0, 1), (0, 1, 0), (0, 1, 1))
    FLIP = ((0, 0, 1), (0, 1, 0), (1, 0, 0), (0, 1, 1), (1, 0, 1), (1, 1, 0), (1, 1, 1))

    def ag_dev(i, kind):
        p1, p2, q1, q2, base = place(i)
        if kind == 0:
            return px
        return {"outer": p2 if kind in (1, 3) else p1}

    def ag_copy(i, kind, src=None):
        row = ag_row(i, *KIND[kind])
        return remote(row if src is None else src, row, ag_s.at[i * 7 + kind], ag_r.at[i * 7 + kind], ag_dev(i, kind))

    def ag_in(i, kind):
        row = ag_row(i, *FLIP[kind])
        return remote(row, row, ag_s.at[i * 7 + kind], ag_r.at[i * 7 + kind], ag_dev(i, kind))

    def own_fin(i):
        return pltpu.make_async_copy(FIN.at[ds16(i * 16, 16), :], ag_row(i, 0, 0, 0), loc.at[3 + i])

    def stage4(i):
        rsx_copy(i).wait_recv()
        total = three(i, xh * 16) + RSX[ds16(i * 16, 16), :].astype(F32)
        high = total.astype(BF16)
        low = (total - high.astype(F32)).astype(BF16)
        both = jnp.concatenate([high, low], axis=0)
        pieces = []
        for b in range(DCOL // BLOCK):
            r = dot(both[:, b * BLOCK:(b + 1) * BLOCK], S)
            pieces.append(((r[:16] + r[16:]) * (BLOCK ** (-0.5))).astype(BF16))
        FIN[ds16(i * 16, 16), :] = jnp.concatenate(pieces, axis=1)
        for kind in range(3):
            ag_copy(i, kind, FIN.at[ds16(i * 16, 16), :]).start()
        own_fin(i).start()

    def stage5(i):
        ag_in(i, 0).wait_recv()
        ag_copy(i, 3).start()
        ag_copy(i, 4).start()

    def stage6(i):
        ag_in(i, 1).wait_recv()
        ag_copy(i, 5).start()
        ag_in(i, 3).wait_recv()
        ag_copy(i, 6).start()

    def stage7(i):
        for kind in (2, 4, 5, 6):
            ag_in(i, kind).wait_recv()

    for ch in range(2):
        weight(ch)
        rs1_copy(ch * 2).start()
        rs1_copy(ch * 2 + 1).start()
    for dz in (4, 1, -1):
        out_stage(zat(dz))

    combos(stage2)
    out_in(sib).wait_recv()
    orl_copy(sib).start()
    out_relay(3)
    combos(stage3)
    out_relay(2)
    combos(stage4)
    out_relay(1)
    combos(stage5)
    combos(stage6)
    out_relay(4)
    combos(stage7)

    def all_j(body):
        def step(k, carry):
            body(k)
            return carry
        lax.fori_loop(0, 2 * NZ, step, 0)

    all_j(lambda j: orl_in(j).wait_recv())
    own_out.wait()
    for half in range(2):
        for direction in range(2):
            for step in range(4):
                if step < 3 or (direction, half) in LAST:
                    ring(direction, step, half).wait_send()
    for dz in range(NZ):
        sib_copy(dz, c).wait_send()
    sib_att().wait_send()
    out_copy(sib).wait_send()
    for dz in range(1, 5):
        def body(j):
            att_copy(j).wait_send()
            arl_copy(j).wait_send()
            out_copy(j).wait_send()
        over(dz, body)
    all_j(lambda j: orl_copy(j).wait_send())

    def parts(zz, carry):
        par_copy(zz).wait_send()
        return carry

    lax.fori_loop(0, NZ, parts, 0)

    def sums(i):
        rs1_copy(i).wait_send()
        rs2_copy(i).wait_send()
        rsx_copy(i).wait_send()
        for kind in range(7):
            ag_copy(i, kind).wait_send()
        own_fin(i).wait()

    combos(sums)


def local(attn_out, cotangent, out_weight):
    hbm, vmem = pl.BlockSpec(memory_space=pl.ANY), pl.BlockSpec(memory_space=pltpu.VMEM)
    dma = pltpu.SemaphoreType.DMA
    tokens = TOK * 2 * NZ
    return pl.pallas_call(
        kernel,
        out_shape=(jax.ShapeDtypeStruct(attn_out.shape, BF16), jax.ShapeDtypeStruct(out_weight.shape, BF16)),
        in_specs=[hbm, vmem, hbm],
        out_specs=(hbm, hbm),
        scratch_shapes=[
            pltpu.VMEM((tokens, DCOL), BF16),
            pltpu.VMEM((HROW, DCOL), BF16),
            pltpu.VMEM((DCOL, HROW), BF16),
            pltpu.VMEM((tokens, HROW), BF16),
            pltpu.VMEM((HROW, tokens), BF16),
            pltpu.VMEM((tokens, HALF), F32),
            pltpu.VMEM((tokens, HALF), BF16),
            pltpu.VMEM((tokens, HALF), BF16),
            pltpu.VMEM((tokens, HALF), BF16),
            pltpu.VMEM((HROW, DCOL), BF16),
            pltpu.VMEM((256, DCOL), BF16),
            pltpu.VMEM((128, DCOL), BF16),
            pltpu.VMEM((64, DCOL), BF16),
            pltpu.VMEM((128, DCOL), BF16),
            pltpu.VMEM((64, DCOL), BF16),
            pltpu.VMEM((64, DCOL), BF16),
            dma((16,)), dma((16,)),
            dma((NZ,)), dma((NZ,)),
            dma((16,)), dma((16,)),
            dma((16,)), dma((16,)),
            dma((NZ,)), dma((NZ,)),
            dma((16,)), dma((16,)),
            dma((16,)), dma((16,)),
            dma((12,)), dma((12,)),
            dma((28,)), dma((28,)),
            dma((7,)),
        ],
        compiler_params=pltpu.CompilerParams(
            collective_id=0, has_side_effects=True, vmem_limit_bytes=48 * 1024 * 1024),
    )(attn_out, cotangent, out_weight)


def solution(mesh):
    in_specs = (P(("outer", "dp"), None), P(("outer", "dp"), "tensor"), P("dp", "tensor"))
    out_specs = (P(("outer", "dp"), None), P("dp", "tensor"))
    return jax.shard_map(local, mesh=mesh, in_specs=in_specs, out_specs=out_specs, check_vma=False)
```

time: 347 us -> 144 us (0.41)
  waiting for transfers between devices: 273 us -> 0 us
  Pallas kernels: 0 us -> 140 us
  matrix products: 25.7 us -> 0 us
  starting transfers between devices: 18 us -> 0 us
  between operations: 13.8 us -> 0.65 us
  local copies, waits for them, and re-layouts: 15 us -> 3.67 us
    psum x2 -> x0, waiting for transfers between devices: 182 us -> none  [the longest x1 112 us: local(): total = lax.psum(rotated.astype(jnp.bfloat16), 'outer').astype(jnp.float32)]
    pallas_call x0 -> x1, Pallas kernels: none -> 140 us  [local(): pl.pallas_call(kernel, out_shape=(jax.ShapeDtypeStruct(attn_out.shape, BF...]
    all_gather x1 -> x0, waiting for transfers between devices: 90.1 us -> none  [local(): cot_pod = lax.all_gather(cotangent, 'dp', axis=0, tiled=True)]
    dot_general x4 -> x0, matrix products: 25.7 us -> none  [the longest x1 9.15 us: local(): lax.dot_general(cot_pod, out_weight, (((1,), (1,)), ((), ())), preferred_...]
    all_to_all x2 -> x0, starting transfers between devices: 17.7 us -> none  [the longest x1 9.98 us: local(): lax.all_to_all(attn_out, 'dp', split_axis=1, concat_axis=0, tiled=True)]
    all_to_all x2 -> x0, local copies, waits for them, and re-layouts: 7.05 us -> none  [the longest x1 3.92 us: local(): lax.all_to_all(attn_out, 'dp', split_axis=1, concat_axis=0, tiled=True)]
    unnamed x4, local copies, waits for them, and re-layouts: 7.99 us -> 3.67 us
  transfers between devices with their start and end apart: 5 -> 0, of which waited for: 3 -> 0; matrix products, arithmetic and copies ran while one was open for 11% -> 0% of each run, Pallas kernels for 0% -> 0%
where the time goes in v1:
time: 144 us
  Pallas kernels  140 us (97%)
  local copies, waits for them, and re-layouts  3.67 us (3%)
    pallas_call x1, Pallas kernels, local(): pl.pallas_call(kernel, out_shape=(jax.ShapeDtypeStruct(attn_out.shape, BF...  140 us
    unnamed x4, local copies, waits for them, and re-layouts  3.67 us

profile of v1, /device:TPU:1, one launch (start us, length us, event | category | flops | bytes accessed | tf_op | source)
XLA Modules:
  0.0 144.3 jit_solution(9865780019060515175)
XLA Ops:
  0.6 0.0 copy-start
  0.6 1.0 copy-done
  1.7 140.0 %shard_map.50 = (bf16[128,8192]{1,0:T(8,128)(2,1)S(1)}, bf16[512,2048]{1,0:T(8,128)(2,1)S(1)}) custom-call(bf16[128,8192]{1,0:T(8,128)(2,1)} %attn.1, bf16[128,2048]{1,0:T(8,128)(2,1)S(1)} %copy-done, bf16[512,2048]{1,0:T(8,128)(2,1)} %w.1), custom_call_target="tpu_custom_call" | custom-call | tf_op jit(solution)/shard_map/pallas_call | solution.py:448
  141.7 1.3 copy.7
  143.0 1.3 copy.8
Async XLA Ops:
  0.6 1.0 copy-start

commit v2 on v1

--- a/solution.py
+++ b/solution.py
@@ -15,6 +15,8 @@
 DCOL = 2048
 HROW = 512
 HALF = 256
+NCH = 4
+CW = DCOL // NCH
 CLIP = 2.5
 
 
@@ -32,7 +34,7 @@
     return jnp.dot(a, b, preferred_element_type=F32)
 
 
-def kernel(attn, cot, w, out, outw, COT, WV, WRT, ACT, AT, PART, PSEND, PRECV, OSEND, WG, RS1, RS2, RSX, S2, SX, FIN,
+def kernel(attn, cot, w, out, outw, COTIN, COT, WV, WRT, ACT, AT, PART, PSEND, PRECV, OSEND, WG, RS1, RS2, RSX, S2, SX, FIN,
            ring_s, ring_r, sib_s, sib_r, att_s, att_r, arl_s, arl_r, par_s, par_r, out_s, out_r, orl_s, orl_r,
            rs_s, rs_r, ag_s, ag_r, loc):
     outer, me, t = lax.axis_index("outer"), lax.axis_index("dp"), lax.axis_index("tensor")
@@ -77,30 +79,35 @@
         attn.at[:, pl.ds(pl.multiple_of(me * HROW, HROW), HROW)], rows(ACT, me * TOK, TOK), loc.at[1])
     own_act.start()
 
+    load_cot = pltpu.make_async_copy(cot, COTIN, loc.at[3])
+    load_cot.start()
     S = signs()
+    load_cot.wait()
     for b in range(DCOL // BLOCK):
-        part = slice(b * BLOCK, (b + 1) * BLOCK)
-        COT[pl.ds(pl.multiple_of(me * TOK, TOK), TOK), part] = (dot(cot[:, part], S) * 0.125).astype(BF16)
+        k, inside = b * BLOCK // CW, b * BLOCK % CW
+        turned = dot(COTIN[:, b * BLOCK:(b + 1) * BLOCK], S) * 0.125
+        COT[k, pl.ds(pl.multiple_of(me * TOK, TOK), TOK), inside:inside + BLOCK] = turned.astype(BF16)
 
     pl.semaphore_wait(barrier, 2 * NZ - 1 + 4)
 
-    def ring(direction, step, half):
+    def goes(direction, step, half):
+        return step < 3 or direction == half
+
+    def ring_block(direction, k, step, half, target_step):
         sgn = 1 - 2 * direction
-        block = rows(COT, (zat(-sgn * step) * 2 + c) * TOK + half * 64, 64)
-        at = direction * 8 + step * 2 + half
+        at = ((direction * NCH + k) * 4 + step) * 2 + half
+        block = rows(COT.at[k], (zat(-sgn * target_step) * 2 + c) * TOK + half * 64, 64)
         return remote(block, block, ring_s.at[at], ring_r.at[at], zdev(zat(sgn) * 2 + c))
 
-    def ring_in(direction, step, half):
-        sgn = 1 - 2 * direction
-        block = rows(COT, (zat(-sgn * (step + 1)) * 2 + c) * TOK + half * 64, 64)
-        at = direction * 8 + step * 2 + half
-        return remote(block, block, ring_s.at[at], ring_r.at[at], zdev(zat(sgn) * 2 + c))
-
-    LAST = ((0, 0), (1, 1))
-
-    def sib_copy(dz, core):
-        at = dz % NZ
-        block = rows(COT, (zat(dz) * 2 + core) * TOK, TOK)
+    def ring(direction, k, step, half):
+        return ring_block(direction, k, step, half, step)
+
+    def ring_in(direction, k, step, half):
+        return ring_block(direction, k, step, half, step + 1)
+
+    def sib_copy(k, dz, core):
+        at = k * NZ + dz % NZ
+        block = rows(COT.at[k], (zat(dz) * 2 + core) * TOK, TOK)
         return remote(block, block, sib_s.at[at], sib_r.at[at], zdev(sib))
 
     def other(k, dz):
@@ -162,10 +169,14 @@
 
     def process(zz):
         at = pl.ds(pl.multiple_of(zz * HALF, HALF), HALF)
-        x = COT[at, :]
-        PSEND[at, :] = dot(x, WRT[:, pl.ds(pl.multiple_of((1 - t) * HALF, HALF), HALF)]).astype(BF16)
+
+        def half(which):
+            columns = pl.ds(pl.multiple_of(which * HALF, HALF), HALF)
+            return sum(dot(COT[k, at, :], WRT[k * CW:(k + 1) * CW, columns]) for k in range(NCH))
+
+        PSEND[at, :] = half(1 - t).astype(BF16)
         par_copy(zz).start()
-        PART[at, :] = dot(x, WRT[:, pl.ds(pl.multiple_of(t * HALF, HALF), HALF)])
+        PART[at, :] = half(t)
 
     def mine(j):
         return out.at[:, pl.ds(pl.multiple_of(j * HROW + t * HALF, HALF), HALF)]
@@ -203,74 +214,22 @@
             orl_copy(j).start()
         over(dz, body)
 
-    for half in range(2):
-        for direction in range(2):
-            ring(direction, 0, half).start()
-    sib_copy(0, c).start()
-    sib_att().start()
-    att_send(4)
-
-    load_w.wait()
-    for b in range(DCOL // BLOCK):
-        part = slice(b * BLOCK, (b + 1) * BLOCK)
-        turned = lax.dot_general(S, WV[:, part], (((0,), (1,)), ((), ())), preferred_element_type=F32)
-        WRT[part, :] = (turned * 0.0625).astype(BF16)
-    sib_copy(0, 1 - c).wait_recv()
-    process(z)
-    own_act.wait()
-    turn(me)
-
-    for step in range(1, 4):
-        for half in range(2):
-            for direction in range(2):
-                ring_in(direction, step - 1, half).wait_recv()
-                if step < 3 or (direction, half) in LAST:
-                    ring(direction, step, half).start()
-        sib_copy(-step, c).start()
-        sib_copy(step, c).start()
-        att_send(4 - step)
-        att_relay(5 - step)
-        if step == 1:
-            sib_att_in().wait_recv()
-            turn(sib)
-        else:
-            att_finish(6 - step)
-        sib_copy(-step, 1 - c).wait_recv()
-        process(zat(-step))
-        sib_copy(step, 1 - c).wait_recv()
-        process(zat(step))
-
-    for direction, half in LAST:
-        ring_in(direction, 3, half).wait_recv()
-    sib_copy(4, c).start()
-    att_relay(1)
-    out_sum(z)
-    own_out.start()
-    out_copy(sib).start()
-    orl_copy(me, rows(OSEND, me * TOK, TOK)).start()
-    att_finish(2)
-    sib_copy(4, 1 - c).wait_recv()
-    process(zat(4))
-    for dz in (3, -3, 2, -2):
-        out_stage(zat(dz))
-    att_finish(1)
-
     ones = jnp.ones((BLOCK, BLOCK), BF16)
     scale = factor * 8.0 * BLOCK ** (-0.5)
 
-    def weight(ch):
+    def weight(k):
         def piece(n, carry):
-            at = pl.multiple_of(n * 512, 512)
-            acc = dot(AT[ch * HALF:(ch + 1) * HALF, :], COT[:, pl.ds(at, 512)]) * scale
+            at = pl.multiple_of(n * HALF, HALF)
+            acc = dot(AT[pl.ds(at, HALF), :], COT[k]) * scale
             clipped = []
-            for b in range(4):
+            for b in range(CW // BLOCK):
                 x = acc[:, b * BLOCK:(b + 1) * BLOCK]
                 mean = dot((x * x).astype(BF16), ones) * (1.0 / BLOCK)
                 limit = CLIP * jnp.sqrt(mean + 1e-6)
                 clipped.append(jnp.clip(x, -limit, limit).astype(BF16))
-            WG[ch * HALF:(ch + 1) * HALF, pl.ds(at, 512)] = jnp.concatenate(clipped, axis=1)
+            WG[pl.ds(pl.multiple_of(k * HROW + n * HALF, HALF), HALF), :] = jnp.concatenate(clipped, axis=1)
             return carry
-        lax.fori_loop(0, DCOL // 512, piece, 0)
+        lax.fori_loop(0, HROW // HALF, piece, 0)
 
     def pick(half, a, b):
         return (1 - half) * a + half * b
@@ -278,7 +237,7 @@
     def place(i):
         half = i % 2
         p1, p2 = pick(half, y1, y3) * 2 + xh, pick(half, y3, y1) * 2 + xh
-        return p1, p2, pick(half, b1, b2), pick(half, b2, b1), i * 128
+        return p1, p2, pick(half, b1, b2), pick(half, b2, b1), i * 256
 
     px = {"outer": y * 2 + 1 - xh}
 
@@ -287,39 +246,37 @@
 
     def rs1_copy(i):
         p1, p2, q1, q2, base = place(i)
-        return remote(WG.at[ds16(base + (1 - q1) * 64, 64), :], RS1.at[ds16(i * 64, 64), :],
+        return remote(WG.at[ds16(base + (1 - q1) * 128, 128), :], RS1.at[ds16(i * 128, 128), :],
                       rs_s.at[i], rs_r.at[i], {"outer": p1})
 
     def rs2_copy(i):
         p1, p2, q1, q2, base = place(i)
-        return remote(S2.at[ds16(i * 32, 32), :], RS2.at[ds16(i * 32, 32), :], rs_s.at[4 + i], rs_r.at[4 + i], {"outer": p2})
+        return remote(S2.at[ds16(i * 64, 64), :], RS2.at[ds16(i * 64, 64), :], rs_s.at[8 + i], rs_r.at[8 + i], {"outer": p2})
 
     def rsx_copy(i):
-        return remote(SX.at[ds16(i * 16, 16), :], RSX.at[ds16(i * 16, 16), :], rs_s.at[8 + i], rs_r.at[8 + i], px)
-
-    def combos(body):
-        def step(i, carry):
-            body(i)
-            return carry
-        lax.fori_loop(0, 4, step, 0)
+        return remote(SX.at[ds16(i * 32, 32), :], RSX.at[ds16(i * 32, 32), :], rs_s.at[16 + i], rs_r.at[16 + i], px)
+
+    def combos(body, k):
+        body(2 * k)
+        body(2 * k + 1)
 
     def stage2(i):
         p1, p2, q1, q2, base = place(i)
         rs1_copy(i).wait_recv()
-        off = (1 - q2) * 32
-        S2[ds16(i * 32, 32), :] = (WG[ds16(base + q1 * 64 + off, 32), :].astype(F32)
-                                   + RS1[ds16(i * 64 + off, 32), :].astype(F32)).astype(BF16)
+        off = (1 - q2) * 64
+        S2[ds16(i * 64, 64), :] = (WG[ds16(base + q1 * 128 + off, 64), :].astype(F32)
+                                   + RS1[ds16(i * 128 + off, 64), :].astype(F32)).astype(BF16)
         rs2_copy(i).start()
 
     def three(i, row):
         p1, p2, q1, q2, base = place(i)
-        return (WG[ds16(base + q1 * 64 + q2 * 32 + row, 16), :].astype(F32)
-                + RS1[ds16(i * 64 + q2 * 32 + row, 16), :].astype(F32)
-                + RS2[ds16(i * 32 + row, 16), :].astype(F32))
+        return (WG[ds16(base + q1 * 128 + q2 * 64 + row, 32), :].astype(F32)
+                + RS1[ds16(i * 128 + q2 * 64 + row, 32), :].astype(F32)
+                + RS2[ds16(i * 64 + row, 32), :].astype(F32))
 
     def stage3(i):
         rs2_copy(i).wait_recv()
-        SX[ds16(i * 16, 16), :] = three(i, (1 - xh) * 16).astype(BF16)
+        SX[ds16(i * 32, 32), :] = three(i, (1 - xh) * 32).astype(BF16)
         rsx_copy(i).start()
 
     def ag_row(i, f1, f2, fx):
@@ -327,7 +284,7 @@
         a = q1 if f1 == 0 else 1 - q1
         b = q2 if f2 == 0 else 1 - q2
         d = xh if fx == 0 else 1 - xh
-        return outw.at[ds16(base + a * 64 + b * 32 + d * 16, 16), :]
+        return outw.at[ds16(i % 2 * 256 + a * 128 + b * 64 + d * 32, 32), pl.ds(pl.multiple_of(i // 2 * CW, CW), CW)]
 
     KIND = ((0, 0, 0), (0, 0, 0), (0, 0, 0), (0, 0, 1), (0, 0, 1), (0, 1, 0), (0, 1, 1))
     FLIP = ((0, 0, 1), (0, 1, 0), (1, 0, 0), (0, 1, 1), (1, 0, 1), (1, 1, 0), (1, 1, 1))
@@ -347,21 +304,21 @@
         return remote(row, row, ag_s.at[i * 7 + kind], ag_r.at[i * 7 + kind], ag_dev(i, kind))
 
     def own_fin(i):
-        return pltpu.make_async_copy(FIN.at[ds16(i * 16, 16), :], ag_row(i, 0, 0, 0), loc.at[3 + i])
+        return pltpu.make_async_copy(FIN.at[ds16(i * 32, 32), :], ag_row(i, 0, 0, 0), loc.at[4 + i])
 
     def stage4(i):
         rsx_copy(i).wait_recv()
-        total = three(i, xh * 16) + RSX[ds16(i * 16, 16), :].astype(F32)
+        total = three(i, xh * 32) + RSX[ds16(i * 32, 32), :].astype(F32)
         high = total.astype(BF16)
         low = (total - high.astype(F32)).astype(BF16)
         both = jnp.concatenate([high, low], axis=0)
         pieces = []
-        for b in range(DCOL // BLOCK):
+        for b in range(CW // BLOCK):
             r = dot(both[:, b * BLOCK:(b + 1) * BLOCK], S)
-            pieces.append(((r[:16] + r[16:]) * (BLOCK ** (-0.5))).astype(BF16))
-        FIN[ds16(i * 16, 16), :] = jnp.concatenate(pieces, axis=1)
+            pieces.append(((r[:32] + r[32:]) * (BLOCK ** (-0.5))).astype(BF16))
+        FIN[ds16(i * 32, 32), :] = jnp.concatenate(pieces, axis=1)
         for kind in range(3):
-            ag_copy(i, kind, FIN.at[ds16(i * 16, 16), :]).start()
+            ag_copy(i, kind, FIN.at[ds16(i * 32, 32), :]).start()
         own_fin(i).start()
 
     def stage5(i):
@@ -379,25 +336,102 @@
         for kind in (2, 4, 5, 6):
             ag_in(i, kind).wait_recv()
 
-    for ch in range(2):
-        weight(ch)
-        rs1_copy(ch * 2).start()
-        rs1_copy(ch * 2 + 1).start()
-    for dz in (4, 1, -1):
-        out_stage(zat(dz))
-
-    combos(stage2)
-    out_in(sib).wait_recv()
-    orl_copy(sib).start()
+    def send_ring(k, step):
+        for half in range(2):
+            for direction in range(2):
+                if step and goes(direction, step - 1, half):
+                    ring_in(direction, k, step - 1, half).wait_recv()
+                if step < 4 and goes(direction, step, half):
+                    ring(direction, k, step, half).start()
+        for dz in ((0,) if step == 0 else (4,) if step == 4 else (-step, step)):
+            sib_copy(k, dz, c).start()
+
+    def sib_wait(k, step):
+        for dz in ((0,) if step == 0 else (4,) if step == 4 else (-step, step)):
+            sib_copy(k, dz, 1 - c).wait_recv()
+
+    SKEW = (0, 0, 3, 3)
+
+    def slot_items(slot):
+        return [(k, slot - SKEW[k]) for k in range(NCH) if 0 <= slot - SKEW[k] <= 4]
+
+    ORDER = (4, 3, 2, 1)
+
+    def reduce_stage(k):
+        for i in (2 * k, 2 * k + 1):
+            rs1_copy(i).start()
+
+    def chain(slot, first):
+        for k in range(NCH):
+            a = slot - first[k]
+            if 1 <= a <= 5:
+                combos((stage2, stage3, stage4, stage5, stage6)[a - 1], k)
+
+    FIRST = tuple(max(5, at + 4) for at in SKEW)
+    END = SKEW[-1] + 4
+
+    for slot in range(END + 1):
+        for k, step in slot_items(slot):
+            send_ring(k, step)
+        if slot < 4:
+            att_send(ORDER[slot])
+        if slot == 0:
+            sib_att().start()
+            load_w.wait()
+            for b in range(DCOL // BLOCK):
+                part = slice(b * BLOCK, (b + 1) * BLOCK)
+                turned = lax.dot_general(S, WV[:, part], (((0,), (1,)), ((), ())), preferred_element_type=F32)
+                WRT[part, :] = (turned * 0.0625).astype(BF16)
+            own_act.wait()
+            turn(me)
+            sib_att_in().wait_recv()
+            turn(sib)
+        if 1 <= slot <= 4:
+            att_relay(ORDER[slot - 1])
+        if 2 <= slot <= 5:
+            att_finish(ORDER[slot - 2])
+        if slot < END:
+            chain(slot, FIRST)
+        for k, step in slot_items(slot):
+            sib_wait(k, step)
+        for k in range(NCH):
+            if slot == FIRST[k]:
+                weight(k)
+                reduce_stage(k)
+        if slot == END:
+            chain(slot, FIRST)
+        if slot == END - 3:
+            process(z)
+        if slot >= END - 3:
+            step = slot - END + 4
+            for dz in ((4,) if step == 4 else (-step, step)):
+                process(zat(dz))
+        if slot == END - 2:
+            out_sum(z)
+            own_out.start()
+            out_copy(sib).start()
+            orl_copy(me, rows(OSEND, me * TOK, TOK)).start()
+        if slot == END - 1:
+            out_stage(zat(1))
+            out_stage(zat(-1))
+        if slot == END:
+            for dz in (2, -2, 3, -3):
+                out_stage(zat(dz))
+            out_in(sib).wait_recv()
+            orl_copy(sib).start()
+
+    chain(END + 1, FIRST)
+    out_stage(zat(4))
+    out_relay(1)
+    chain(END + 2, FIRST)
+    chain(END + 3, FIRST)
+    out_relay(2)
+    chain(END + 4, FIRST)
+    chain(END + 5, FIRST)
     out_relay(3)
-    combos(stage3)
-    out_relay(2)
-    combos(stage4)
-    out_relay(1)
-    combos(stage5)
-    combos(stage6)
     out_relay(4)
-    combos(stage7)
+    for k in range(NCH):
+        combos(stage7, k)
 
     def all_j(body):
         def step(k, carry):
@@ -407,13 +441,14 @@
 
     all_j(lambda j: orl_in(j).wait_recv())
     own_out.wait()
-    for half in range(2):
+    for k in range(NCH):
         for direction in range(2):
             for step in range(4):
-                if step < 3 or (direction, half) in LAST:
-                    ring(direction, step, half).wait_send()
-    for dz in range(NZ):
-        sib_copy(dz, c).wait_send()
+                for half in range(2):
+                    if goes(direction, step, half):
+                        ring(direction, k, step, half).wait_send()
+        for dz in range(NZ):
+            sib_copy(k, dz, c).wait_send()
     sib_att().wait_send()
     out_copy(sib).wait_send()
     for dz in range(1, 5):
@@ -438,20 +473,21 @@
             ag_copy(i, kind).wait_send()
         own_fin(i).wait()
 
-    combos(sums)
+    lax.fori_loop(0, 2 * NCH, lambda i, carry: (sums(i), carry)[1], 0)
 
 
 def local(attn_out, cotangent, out_weight):
-    hbm, vmem = pl.BlockSpec(memory_space=pl.ANY), pl.BlockSpec(memory_space=pltpu.VMEM)
+    hbm = pl.BlockSpec(memory_space=pl.ANY)
     dma = pltpu.SemaphoreType.DMA
     tokens = TOK * 2 * NZ
     return pl.pallas_call(
         kernel,
         out_shape=(jax.ShapeDtypeStruct(attn_out.shape, BF16), jax.ShapeDtypeStruct(out_weight.shape, BF16)),
-        in_specs=[hbm, vmem, hbm],
+        in_specs=[hbm, hbm, hbm],
         out_specs=(hbm, hbm),
         scratch_shapes=[
-            pltpu.VMEM((tokens, DCOL), BF16),
+            pltpu.VMEM((TOK, DCOL), BF16),
+            pltpu.VMEM((NCH, tokens, CW), BF16),
             pltpu.VMEM((HROW, DCOL), BF16),
             pltpu.VMEM((DCOL, HROW), BF16),
             pltpu.VMEM((tokens, HROW), BF16),
@@ -460,23 +496,23 @@
             pltpu.VMEM((tokens, HALF), BF16),
             pltpu.VMEM((tokens, HALF), BF16),
             pltpu.VMEM((tokens, HALF), BF16),
-            pltpu.VMEM((HROW, DCOL), BF16),
-            pltpu.VMEM((256, DCOL), BF16),
-            pltpu.VMEM((128, DCOL), BF16),
-            pltpu.VMEM((64, DCOL), BF16),
-            pltpu.VMEM((128, DCOL), BF16),
-            pltpu.VMEM((64, DCOL), BF16),
-            pltpu.VMEM((64, DCOL), BF16),
-            dma((16,)), dma((16,)),
-            dma((NZ,)), dma((NZ,)),
+            pltpu.VMEM((NCH * HROW, CW), BF16),
+            pltpu.VMEM((1024, CW), BF16),
+            pltpu.VMEM((512, CW), BF16),
+            pltpu.VMEM((256, CW), BF16),
+            pltpu.VMEM((512, CW), BF16),
+            pltpu.VMEM((256, CW), BF16),
+            pltpu.VMEM((256, CW), BF16),
+            dma((64,)), dma((64,)),
+            dma((NCH * NZ,)), dma((NCH * NZ,)),
             dma((16,)), dma((16,)),
             dma((16,)), dma((16,)),
             dma((NZ,)), dma((NZ,)),
             dma((16,)), dma((16,)),
             dma((16,)), dma((16,)),
-            dma((12,)), dma((12,)),
-            dma((28,)), dma((28,)),
-            dma((7,)),
+            dma((24,)), dma((24,)),
+            dma((56,)), dma((56,)),
+            dma((12,)),
         ],
         compiler_params=pltpu.CompilerParams(
             collective_id=0, has_side_effects=True, vmem_limit_bytes=48 * 1024 * 1024),

time: 144 us -> 133 us (0.924)
  Pallas kernels: 140 us -> 129 us
    pallas_call x1, Pallas kernels: 140 us -> 129 us  [local(): pl.pallas_call(kernel, out_shape=(jax.ShapeDtypeStruct(attn_out.shape, BF...]
where the time goes in v2:
time: 133 us
  Pallas kernels  129 us (97%)
  local copies, waits for them, and re-layouts  3.67 us (3%)
    pallas_call x1, Pallas kernels, local(): pl.pallas_call(kernel, out_shape=(jax.ShapeDtypeStruct(attn_out.shape, BF...  129 us
    unnamed x4, local copies, waits for them, and re-layouts  3.67 us

profile of v2, /device:TPU:1, one launch (start us, length us, event | category | flops | bytes accessed | tf_op | source)
XLA Modules:
  0.0 132.9 jit_solution(3087828061988430813)
XLA Ops:
  0.6 0.0 copy-start
  0.6 1.0 copy-done
  1.7 128.6 %shard_map.50 = (bf16[128,8192]{1,0:T(8,128)(2,1)S(1)}, bf16[512,2048]{1,0:T(8,128)(2,1)S(1)}) custom-call(bf16[128,8192]{1,0:T(8,128)(2,1)} %attn.1, bf16[128,2048]{1,0:T(8,128)(2,1)S(1)} %copy-done, bf16[512,2048]{1,0:T(8,128)(2,1)} %w.1), custom_call_target="tpu_custom_call" | custom-call | tf_op jit(solution)/shard_map/pallas_call | solution.py:483
  130.2 1.3 copy.7
  131.6 1.3 copy.8
Async XLA Ops:
  0.6 1.0 copy-start

commit v3 on v2

--- a/solution.py
+++ b/solution.py
@@ -254,7 +254,7 @@
         return remote(S2.at[ds16(i * 64, 64), :], RS2.at[ds16(i * 64, 64), :], rs_s.at[8 + i], rs_r.at[8 + i], {"outer": p2})
 
     def rsx_copy(i):
-        return remote(SX.at[ds16(i * 32, 32), :], RSX.at[ds16(i * 32, 32), :], rs_s.at[16 + i], rs_r.at[16 + i], px)
+        return remote(SX.at[ds16(i * 64, 64), :], RSX.at[ds16(i * 64, 64), :], rs_s.at[16 + i], rs_r.at[16 + i], px)
 
     def combos(body, k):
         body(2 * k)
@@ -268,72 +268,58 @@
                                    + RS1[ds16(i * 128 + off, 64), :].astype(F32)).astype(BF16)
         rs2_copy(i).start()
 
-    def three(i, row):
-        p1, p2, q1, q2, base = place(i)
-        return (WG[ds16(base + q1 * 128 + q2 * 64 + row, 32), :].astype(F32)
-                + RS1[ds16(i * 128 + q2 * 64 + row, 32), :].astype(F32)
-                + RS2[ds16(i * 64 + row, 32), :].astype(F32))
-
     def stage3(i):
+        p1, p2, q1, q2, base = place(i)
         rs2_copy(i).wait_recv()
-        SX[ds16(i * 32, 32), :] = three(i, (1 - xh) * 32).astype(BF16)
+        SX[ds16(i * 64, 64), :] = (WG[ds16(base + q1 * 128 + q2 * 64, 64), :].astype(F32)
+                                   + RS1[ds16(i * 128 + q2 * 64, 64), :].astype(F32)
+                                   + RS2[ds16(i * 64, 64), :].astype(F32)).astype(BF16)
         rsx_copy(i).start()
 
-    def ag_row(i, f1, f2, fx):
+    def ag_row(i, f1, f2):
         p1, p2, q1, q2, base = place(i)
         a = q1 if f1 == 0 else 1 - q1
         b = q2 if f2 == 0 else 1 - q2
-        d = xh if fx == 0 else 1 - xh
-        return outw.at[ds16(i % 2 * 256 + a * 128 + b * 64 + d * 32, 32), pl.ds(pl.multiple_of(i // 2 * CW, CW), CW)]
-
-    KIND = ((0, 0, 0), (0, 0, 0), (0, 0, 0), (0, 0, 1), (0, 0, 1), (0, 1, 0), (0, 1, 1))
-    FLIP = ((0, 0, 1), (0, 1, 0), (1, 0, 0), (0, 1, 1), (1, 0, 1), (1, 1, 0), (1, 1, 1))
-
-    def ag_dev(i, kind):
-        p1, p2, q1, q2, base = place(i)
-        if kind == 0:
-            return px
-        return {"outer": p2 if kind in (1, 3) else p1}
+        return outw.at[ds16(i % 2 * 256 + a * 128 + b * 64, 64), pl.ds(pl.multiple_of(i // 2 * CW, CW), CW)]
+
+    KIND = ((0, 0), (0, 0), (0, 1))
+    FLIP = ((0, 1), (1, 0), (1, 1))
 
     def ag_copy(i, kind, src=None):
+        p1, p2, q1, q2, base = place(i)
         row = ag_row(i, *KIND[kind])
-        return remote(row if src is None else src, row, ag_s.at[i * 7 + kind], ag_r.at[i * 7 + kind], ag_dev(i, kind))
+        return remote(row if src is None else src, row, ag_s.at[i * 3 + kind], ag_r.at[i * 3 + kind],
+                      {"outer": p2 if kind == 0 else p1})
 
     def ag_in(i, kind):
+        p1, p2, q1, q2, base = place(i)
         row = ag_row(i, *FLIP[kind])
-        return remote(row, row, ag_s.at[i * 7 + kind], ag_r.at[i * 7 + kind], ag_dev(i, kind))
+        return remote(row, row, ag_s.at[i * 3 + kind], ag_r.at[i * 3 + kind], {"outer": p2 if kind == 0 else p1})
 
     def own_fin(i):
-        return pltpu.make_async_copy(FIN.at[ds16(i * 32, 32), :], ag_row(i, 0, 0, 0), loc.at[4 + i])
+        return pltpu.make_async_copy(FIN.at[ds16(i * 64, 64), :], ag_row(i, 0, 0), loc.at[4 + i])
 
     def stage4(i):
         rsx_copy(i).wait_recv()
-        total = three(i, xh * 32) + RSX[ds16(i * 32, 32), :].astype(F32)
+        total = SX[ds16(i * 64, 64), :].astype(F32) + RSX[ds16(i * 64, 64), :].astype(F32)
         high = total.astype(BF16)
         low = (total - high.astype(F32)).astype(BF16)
         both = jnp.concatenate([high, low], axis=0)
         pieces = []
         for b in range(CW // BLOCK):
             r = dot(both[:, b * BLOCK:(b + 1) * BLOCK], S)
-            pieces.append(((r[:32] + r[32:]) * (BLOCK ** (-0.5))).astype(BF16))
-        FIN[ds16(i * 32, 32), :] = jnp.concatenate(pieces, axis=1)
-        for kind in range(3):
-            ag_copy(i, kind, FIN.at[ds16(i * 32, 32), :]).start()
+            pieces.append(((r[:64] + r[64:]) * (BLOCK ** (-0.5))).astype(BF16))
+        FIN[ds16(i * 64, 64), :] = jnp.concatenate(pieces, axis=1)
+        for kind in range(2):
+            ag_copy(i, kind, FIN.at[ds16(i * 64, 64), :]).start()
         own_fin(i).start()
 
     def stage5(i):
         ag_in(i, 0).wait_recv()
-        ag_copy(i, 3).start()
-        ag_copy(i, 4).start()
-
-    def stage6(i):
-        ag_in(i, 1).wait_recv()
-        ag_copy(i, 5).start()
-        ag_in(i, 3).wait_recv()
-        ag_copy(i, 6).start()
+        ag_copy(i, 2).start()
 
     def stage7(i):
-        for kind in (2, 4, 5, 6):
+        for kind in (1, 2):
             ag_in(i, kind).wait_recv()
 
     def send_ring(k, step):
@@ -355,7 +341,7 @@
     def slot_items(slot):
         return [(k, slot - SKEW[k]) for k in range(NCH) if 0 <= slot - SKEW[k] <= 4]
 
-    ORDER = (4, 3, 2, 1)
+    SENDS = {0: (4,), 1: (3, 2), 2: (1,)}
 
     def reduce_stage(k):
         for i in (2 * k, 2 * k + 1):
@@ -364,17 +350,18 @@
     def chain(slot, first):
         for k in range(NCH):
             a = slot - first[k]
-            if 1 <= a <= 5:
-                combos((stage2, stage3, stage4, stage5, stage6)[a - 1], k)
-
-    FIRST = tuple(max(5, at + 4) for at in SKEW)
+            if 1 <= a <= 4:
+                combos((stage2, stage3, stage4, stage5)[a - 1], k)
+
+    FIRST = (4, 5, 7, 7)
     END = SKEW[-1] + 4
+    SUMS = (END - 2, END - 1, END, END)
 
     for slot in range(END + 1):
         for k, step in slot_items(slot):
             send_ring(k, step)
-        if slot < 4:
-            att_send(ORDER[slot])
+        for dz in SENDS.get(slot, ()):
+            att_send(dz)
         if slot == 0:
             sib_att().start()
             load_w.wait()
@@ -386,20 +373,23 @@
             turn(me)
             sib_att_in().wait_recv()
             turn(sib)
-        if 1 <= slot <= 4:
-            att_relay(ORDER[slot - 1])
-        if 2 <= slot <= 5:
-            att_finish(ORDER[slot - 2])
+        for dz in SENDS.get(slot - 1, ()):
+            att_relay(dz)
+        for dz in SENDS.get(slot - 2, ()):
+            att_finish(dz)
         if slot < END:
-            chain(slot, FIRST)
+            chain(slot, SUMS)
         for k, step in slot_items(slot):
             sib_wait(k, step)
+        if slot == END:
+            out_stage(zat(2))
+            out_stage(zat(-2))
         for k in range(NCH):
             if slot == FIRST[k]:
                 weight(k)
                 reduce_stage(k)
         if slot == END:
-            chain(slot, FIRST)
+            chain(slot, SUMS)
         if slot == END - 3:
             process(z)
         if slot >= END - 3:
@@ -415,32 +405,15 @@
             out_stage(zat(1))
             out_stage(zat(-1))
         if slot == END:
-            for dz in (2, -2, 3, -3):
+            for dz in (3, -3):
                 out_stage(zat(dz))
             out_in(sib).wait_recv()
             orl_copy(sib).start()
 
-    chain(END + 1, FIRST)
     out_stage(zat(4))
     out_relay(1)
-    chain(END + 2, FIRST)
-    chain(END + 3, FIRST)
+    chain(END + 1, SUMS)
     out_relay(2)
-    chain(END + 4, FIRST)
-    chain(END + 5, FIRST)
-    out_relay(3)
-    out_relay(4)
-    for k in range(NCH):
-        combos(stage7, k)
-
-    def all_j(body):
-        def step(k, carry):
-            body(k)
-            return carry
-        lax.fori_loop(0, 2 * NZ, step, 0)
-
-    all_j(lambda j: orl_in(j).wait_recv())
-    own_out.wait()
     for k in range(NCH):
         for direction in range(2):
             for step in range(4):
@@ -450,26 +423,48 @@
         for dz in range(NZ):
             sib_copy(k, dz, c).wait_send()
     sib_att().wait_send()
+
+    def sent(j):
+        att_copy(j).wait_send()
+        arl_copy(j).wait_send()
+
+    for dz in range(1, 5):
+        over(dz, sent)
+
+    def parts(zz, carry):
+        par_copy(zz).wait_send()
+        return carry
+
+    lax.fori_loop(0, NZ, parts, 0)
+
+    chain(END + 2, SUMS)
+    out_relay(3)
+    chain(END + 3, SUMS)
+    out_relay(4)
+    chain(END + 4, SUMS)
+    for k in range(NCH):
+        combos(stage7, k)
+
+    def all_j(body):
+        def step(k, carry):
+            body(k)
+            return carry
+        lax.fori_loop(0, 2 * NZ, step, 0)
+
+    all_j(lambda j: orl_in(j).wait_recv())
+    own_out.wait()
     out_copy(sib).wait_send()
     for dz in range(1, 5):
         def body(j):
-            att_copy(j).wait_send()
-            arl_copy(j).wait_send()
             out_copy(j).wait_send()
         over(dz, body)
     all_j(lambda j: orl_copy(j).wait_send())
-
-    def parts(zz, carry):
-        par_copy(zz).wait_send()
-        return carry
-
-    lax.fori_loop(0, NZ, parts, 0)
 
     def sums(i):
         rs1_copy(i).wait_send()
         rs2_copy(i).wait_send()
         rsx_copy(i).wait_send()
-        for kind in range(7):
+        for kind in range(3):
             ag_copy(i, kind).wait_send()
         own_fin(i).wait()
 
@@ -499,10 +494,10 @@
             pltpu.VMEM((NCH * HROW, CW), BF16),
             pltpu.VMEM((1024, CW), BF16),
             pltpu.VMEM((512, CW), BF16),
-            pltpu.VMEM((256, CW), BF16),
             pltpu.VMEM((512, CW), BF16),
-            pltpu.VMEM((256, CW), BF16),
-            pltpu.VMEM((256, CW), BF16),
+            pltpu.VMEM((512, CW), BF16),
+            pltpu.VMEM((512, CW), BF16),
+            pltpu.VMEM((512, CW), BF16),
             dma((64,)), dma((64,)),
             dma((NCH * NZ,)), dma((NCH * NZ,)),
             dma((16,)), dma((16,)),
@@ -511,7 +506,7 @@
             dma((16,)), dma((16,)),
             dma((16,)), dma((16,)),
             dma((24,)), dma((24,)),
-            dma((56,)), dma((56,)),
+            dma((24,)), dma((24,)),
             dma((12,)),
         ],
         compiler_params=pltpu.CompilerParams(

time: 133 us -> 132 us (level)
  Pallas kernels: 129 us -> 127 us
    pallas_call x1, Pallas kernels: 129 us -> 127 us  [local(): pl.pallas_call(kernel, out_shape=(jax.ShapeDtypeStruct(attn_out.shape, BF...]
where the time goes in v3:
time: 132 us; the launch traced here: 131 us
  Pallas kernels  127 us (96%)
  local copies, waits for them, and re-layouts  3.67 us (3%)
    pallas_call x1, Pallas kernels, local(): pl.pallas_call(kernel, out_shape=(jax.ShapeDtypeStruct(attn_out.shape, BF...  127 us
    unnamed x4, local copies, waits for them, and re-layouts  3.67 us

profile of v3, /device:TPU:1, one launch (start us, length us, event | category | flops | bytes accessed | tf_op | source)
XLA Modules:
  0.0 131.4 jit_solution(2002183115941661694)
XLA Ops:
  0.6 0.0 copy-start
  0.6 1.0 copy-done
  1.7 127.1 %shard_map.50 = (bf16[128,8192]{1,0:T(8,128)(2,1)S(1)}, bf16[512,2048]{1,0:T(8,128)(2,1)S(1)}) custom-call(bf16[128,8192]{1,0:T(8,128)(2,1)} %attn.1, bf16[128,2048]{1,0:T(8,128)(2,1)S(1)} %copy-done, bf16[512,2048]{1,0:T(8,128)(2,1)} %w.1), custom_call_target="tpu_custom_call" | custom-call | tf_op jit(solution)/shard_map/pallas_call | solution.py:478
  128.8 1.3 %copy.7 = bf16[128,8192]{1,0:T(8,128)(2,1)} copy(bf16[128,8192]{1,0:T(8,128)(2,1)S(1)} %get-tuple-element.4) | data formatting | bytes 4194304
  130.1 1.3 %copy.8 = bf16[512,2048]{1,0:T(8,128)(2,1)} copy(bf16[512,2048]{1,0:T(8,128)(2,1)S(1)} %get-tuple-element.5) | data formatting | bytes 4194304
Async XLA Ops:
  0.6 1.0 copy-start

commit v4 on v3

--- a/solution.py
+++ b/solution.py
@@ -341,7 +341,7 @@
     def slot_items(slot):
         return [(k, slot - SKEW[k]) for k in range(NCH) if 0 <= slot - SKEW[k] <= 4]
 
-    SENDS = {0: (4,), 1: (3, 2), 2: (1,)}
+    SENDS = {0: (4,), 1: (3, 2, 1)}
 
     def reduce_stage(k):
         for i in (2 * k, 2 * k + 1):

time: 132 us -> 133 us (level)
  Pallas kernels: 127 us -> 129 us
    pallas_call x1, Pallas kernels: 127 us -> 129 us  [local(): pl.pallas_call(kernel, out_shape=(jax.ShapeDtypeStruct(attn_out.shape, BF...]
where the time goes in v4:
time: 133 us
  Pallas kernels  129 us (97%)
  local copies, waits for them, and re-layouts  3.67 us (3%)
    pallas_call x1, Pallas kernels, local(): pl.pallas_call(kernel, out_shape=(jax.ShapeDtypeStruct(attn_out.shape, BF...  129 us
    unnamed x4, local copies, waits for them, and re-layouts  3.67 us

profile of v4, /device:TPU:1, one launch (start us, length us, event | category | flops | bytes accessed | tf_op | source)
XLA Modules:
  0.0 132.9 jit_solution(2759262731192478773)
XLA Ops:
  0.6 0.0 copy-start
  0.6 1.0 copy-done
  1.7 128.6 %shard_map.50 = (bf16[128,8192]{1,0:T(8,128)(2,1)S(1)}, bf16[512,2048]{1,0:T(8,128)(2,1)S(1)}) custom-call(bf16[128,8192]{1,0:T(8,128)(2,1)} %attn.1, bf16[128,2048]{1,0:T(8,128)(2,1)S(1)} %copy-done, bf16[512,2048]{1,0:T(8,128)(2,1)} %w.1), custom_call_target="tpu_custom_call" | custom-call | tf_op jit(solution)/shard_map/pallas_call | solution.py:478
  130.3 1.3 copy.7
  131.6 1.3 copy.8
Async XLA Ops:
  0.6 1.0 copy-start
